TPU v7x, 32 devices: a whole 2x2x4 slice. The times are simulated.
32 devices in a mesh: groups: 2 (over y), gx: 4 (over z), gy: 2 (over x), gz: 2 (over core).
Axes of the slice: x: 2, y: 2, z: 4, core: 2. Of those that a mesh axis runs over, the one named last changes fastest.
Arguments:
- positions: float32 [3, 4096], P(None, ('groups', 'gx', 'gy', 'gz')), parts along dimension 1, may hold values from 0 to 1
- atom_features: float32 [4096, 64], P(('groups', 'gx', 'gy', 'gz')), parts along dimension 0, may hold values from -6 to 6
- pair_seg: int32 [640, 128], P(('groups', 'gx', 'gy', 'gz')), parts along dimension 0, may hold values from 0 to 31
- pair_other: int32 [640, 128], P(('groups', 'gx', 'gy', 'gz')), parts along dimension 0, may hold values from -1 to 351, as said below
- send_list: int32 [1024], P(('groups', 'gx', 'gy', 'gz')), parts along dimension 0, may hold values from 0 to 127
- radial_w: float32 [2, 64, 8], replicated, may hold values from -2 to 2
- pair_wa: float32 [2, 64, 64], replicated, may hold values from -0.75 to 0.75
- pair_wb: float32 [2, 64, 64], replicated, may hold values from -0.75 to 0.75
- update_w: float32 [2, 64, 192], replicated, may hold values from -0.4375 to 0.4375
- readout: float32 [64], replicated, may hold values from -0.75 to 0.75
Outputs:
- energies: float32 [4096], P(('groups', 'gx', 'gy', 'gz')), parts along dimension 0
- forces: float32 [3, 4096], P(None, ('groups', 'gx', 'gy', 'gz')), parts along dimension 1
There are 2 independent parts, one for each index of `groups`. A program takes and returns all parts, laid end to end along the dimension named above; an argument that names none is the same for every part. Nothing has to cross between parts.
Inputs may be any that keep to these rules, and one draw needn't show every extreme that they name: `pair_other`: -1 marks an empty pair slot; on each domain the share of used slots lies between about 45 and 100 percent.
All inputs are finite; a program needn't handle non-finite values.
Results may differ from a plain program's by a relative error of at most 0.0003.
Values sent between devices are 32-bit elements; how exact they have to be, the bound alone decides.
A program may use at most 128 MiB of HBM per device.

v0:
```python
from functools import partial
import math

import jax
import jax.numpy as jnp
import numpy as np
from jax import lax
from jax.sharding import PartitionSpec as P

CH = 64
SEG = 32
ATOMS = 128


exact = lax.Precision.HIGHEST
cutoff_radius = 4.0
domain_edge = 1.0
soften_square = 0.25
basis_width = 0.5
root_two = math.sqrt(2.0)
parity_sign = np.array([1.0, -1.0, -1.0, -1.0, 1.0, 1.0, 1.0, 1.0, 1.0, 1.0])


def extended_2(block, sides, width):
    for axis, dim in sides:
        count = lax.axis_size(axis)
        forward = [(i, i + 1) for i in range(count - 1)]
        forward.append((count - 1, 0))
        backward = [(target, source) for source, target in forward]
        low = lax.ppermute(
            lax.slice_in_dim(block, block.shape[dim] - width, None, axis=dim), axis, forward
        )
        high = lax.ppermute(lax.slice_in_dim(block, 0, width, axis=dim), axis, backward)
        block = jnp.concatenate([low, block, high], axis=dim)
    return block


def ghost_layout():
    listing = []
    for first in range(4):
        for second in range(4):
            for third in range(4):
                inner = 1 <= first <= 2 and 1 <= second <= 2 and (1 <= third <= 2)
                if not inner:
                    listing.append((first, second, third))
    return listing


def axis_side(padded):
    if padded == 0:
        return (-1, 1)
    if padded == 3:
        return (1, 0)
    return (0, padded - 1)


def ghost_shifts():
    return (
        np.array(
            [[axis_side(padded)[0] for padded in ghost_slot] for ghost_slot in ghost_layout()],
            np.float32,
        )
        * domain_edge
    )


def ghost_indices():
    return np.array(
        [(first * 4 + second) * 4 + third for first, second, third in ghost_layout()], np.int32
    )


def harmonics(unit_vec):
    along_x = unit_vec[:, 0]
    along_y = unit_vec[:, 1]
    along_z = unit_vec[:, 2]
    trace_third = (along_x * along_x + along_y * along_y + along_z * along_z) / 3.0
    return jnp.stack(
        [
            jnp.ones_like(along_x),
            along_x,
            along_y,
            along_z,
            along_x * along_x - trace_third,
            along_y * along_y - trace_third,
            along_z * along_z - trace_third,
            root_two * along_x * along_y,
            root_two * along_x * along_z,
            root_two * along_y * along_z,
        ],
        axis=1,
    )


def pair_weights(separation, proj_centre, proj_partner, radial):
    distance = jnp.sqrt(jnp.sum(separation * separation, axis=1) + soften_square)
    unit_vec = separation / distance[:, None]
    centres = basis_width * (jnp.arange(radial.shape[1]) + 1).astype(jnp.float32)
    scaled = (distance[:, None] - centres[None, :]) / basis_width
    basis_vals = jnp.exp(-scaled * scaled)
    scaled_dist = distance / cutoff_radius
    envelope = (1.0 - scaled_dist * scaled_dist) ** 2
    before = (
        jnp.dot(basis_vals, radial.T, precision=exact, preferred_element_type=jnp.float32)
        + proj_centre
        + proj_partner
    )
    return (envelope[:, None] * jax.nn.silu(before), harmonics(unit_vec))


def layer_env(pos_ext, feat_ext, radial, weight_a, weight_b, pair_seg, pair_other):
    proj_a = jnp.dot(feat_ext, weight_a.T, precision=exact, preferred_element_type=jnp.float32)
    proj_b = jnp.dot(feat_ext, weight_b.T, precision=exact, preferred_element_type=jnp.float32)
    blocks = pair_seg.shape[0]
    block_base = jnp.arange(blocks, dtype=jnp.int32) * (ATOMS - SEG) // (blocks - 1)
    groups = blocks // 4
    seg_groups = pair_seg.reshape(groups, 4, 128)
    other_groups = pair_other.reshape(groups, 4, 128)
    base_groups = block_base.reshape(groups, 4)
    windows = jnp.arange(SEG, dtype=jnp.int32)
    parity = jnp.asarray(np.repeat(parity_sign, CH), jnp.float32)

    def one_group(environment, entries):
        seg_rows, other_rows, base_rows = entries
        centre = (base_rows[:, None] + seg_rows).reshape(-1)
        live_pair = (other_rows >= 0).reshape(-1)
        partner = jnp.maximum(other_rows, 0).reshape(-1)
        separation = pos_ext[partner] - pos_ext[centre]
        weights, angular = pair_weights(separation, proj_a[centre], proj_b[partner], radial)
        weights = jnp.where(live_pair[:, None], weights, 0.0)
        contrib = (angular[:, :, None] * weights[:, None, :]).reshape(-1, 10 * CH)
        selector = (seg_rows[:, :, None] == windows[None, None, :]).astype(jnp.float32)
        summed = jnp.einsum(
            "bps,bpk->bsk", selector, contrib.reshape(4, 128, 10 * CH), precision=exact
        )
        for member in range(4):
            first_row = base_rows[member]
            current = lax.dynamic_slice_in_dim(environment, first_row, SEG, 0)
            environment = lax.dynamic_update_slice_in_dim(
                environment, current + summed[member], first_row, 0
            )
        environment = environment.at[partner].add(contrib * parity[None, :])
        return (environment, None)

    start_env = jnp.zeros((pos_ext.shape[0], 10 * CH), jnp.float32)
    environment, unused = lax.scan(one_group, start_env, (seg_groups, other_groups, base_groups))
    return environment


def update(features, environment, weight):
    shaped = environment.reshape(environment.shape[:-1] + (10, CH))
    scalars = 0.25 * shaped[..., 0, :]
    vectors = 0.1 * jnp.sum(shaped[..., 1:4, :] * shaped[..., 1:4, :], axis=-2)
    tensors = 0.1 * jnp.sum(shaped[..., 4:, :] * shaped[..., 4:, :], axis=-2)
    joined = jnp.concatenate([scalars, vectors, tensors], axis=-1)
    return features + jax.nn.silu(
        jnp.dot(joined, weight.T, precision=exact, preferred_element_type=jnp.float32)
    )


def pick_ghosts(extended):
    flat_rows = extended.reshape((64,) + extended.shape[3:])
    chosen = flat_rows[jnp.asarray(ghost_indices())]
    return chosen.reshape((-1, extended.shape[-1]))


def place_ghosts(ghost_rows):
    columns = ghost_rows.shape[1]
    shaped = ghost_rows.reshape((56, -1, columns))
    frame_rows = jnp.zeros((64,) + shaped.shape[1:], ghost_rows.dtype)
    frame_rows = frame_rows.at[jnp.asarray(ghost_indices())].set(shaped)
    return frame_rows.reshape((4, 4, 4) + shaped.shape[1:])


def gather_slots(extended):
    selected_rows = jnp.asarray(np.array([0, 2, 3, 5], np.int32))
    chosen = extended[selected_rows][:, selected_rows][:, :, selected_rows]
    shaped = chosen.reshape((2, 2, 2, 2, 2, 2) + extended.shape[3:])
    summed = jnp.sum(shaped, axis=(1, 3, 5))
    return summed.reshape((-1, extended.shape[-1]))


def spread_rows(rows, send_list):
    outgoing = rows[send_list].reshape((2, 2, 2, -1, rows.shape[1]))
    arrived = extended_2(outgoing, (("gx", 0), ("gy", 1), ("gz", 2)), 1)
    return pick_ghosts(arrived)


def spread_env_grads(rows, send_list):
    outgoing = rows[send_list].reshape((2, 2, 2, -1, rows.shape[1]))
    arrived = extended_2(outgoing, (("gx", 0), ("gy", 1), ("gz", 2)), 1)
    return pick_ghosts(arrived)


def fold_env(ghost_rows):
    arrived = extended_2(place_ghosts(ghost_rows), (("gx", 0), ("gy", 1), ("gz", 2)), 1)
    return gather_slots(arrived)


def fold_grads(ghost_rows):
    arrived = extended_2(place_ghosts(ghost_rows), (("gx", 0), ("gy", 1), ("gz", 2)), 1)
    return gather_slots(arrived)


def local(
    positions,
    atom_features,
    pair_seg,
    pair_other,
    send_list,
    radial_w,
    pair_wa,
    pair_wb,
    update_w,
    readout,
):
    own_count = atom_features.shape[0]
    own_pos = positions.T
    shift_rows = jnp.repeat(
        jnp.asarray(ghost_shifts(), jnp.float32), send_list.shape[0] // 8, axis=0
    )
    arrived = spread_rows(jnp.concatenate([own_pos, atom_features], axis=1), send_list)
    pos_ext = jnp.concatenate([own_pos, arrived[:, :3] + shift_rows], axis=0)
    first_ext = jnp.concatenate([atom_features, arrived[:, 3:]], axis=0)

    def first_layer(where, features):
        return layer_env(where, features, radial_w[0], pair_wa[0], pair_wb[0], pair_seg, pair_other)

    def second_layer(where, features):
        return layer_env(where, features, radial_w[1], pair_wa[1], pair_wb[1], pair_seg, pair_other)

    env_one, pull_one = jax.vjp(first_layer, pos_ext, first_ext)
    complete_one = env_one[:own_count].at[send_list].add(fold_env(env_one[own_count:]))
    hidden_one, pull_upd_one = jax.vjp(
        partial(update, weight=update_w[0]), atom_features, complete_one
    )
    second_ext = jnp.concatenate([hidden_one, spread_rows(hidden_one, send_list)], axis=0)
    env_two, pull_two = jax.vjp(second_layer, pos_ext, second_ext)
    complete_two = env_two[:own_count].at[send_list].add(fold_env(env_two[own_count:]))
    hidden_two, pull_upd_two = jax.vjp(
        partial(update, weight=update_w[1]), hidden_one, complete_two
    )
    energies = jnp.dot(hidden_two, readout, precision=exact, preferred_element_type=jnp.float32)
    grad_two_h, grad_env_two = pull_upd_two(jnp.broadcast_to(readout, hidden_two.shape))
    env_grad_two = jnp.concatenate(
        [grad_env_two, spread_env_grads(grad_env_two, send_list)], axis=0
    )
    pos_grad_two, feat_grad_two = pull_two(env_grad_two)
    returned = fold_grads(feat_grad_two[own_count:])
    hidden_grad = grad_two_h + feat_grad_two[:own_count].at[send_list].add(returned)
    unused_h, grad_env_one = pull_upd_one(hidden_grad)
    env_grad_one = jnp.concatenate(
        [grad_env_one, spread_env_grads(grad_env_one, send_list)], axis=0
    )
    pos_grad_one, unused_f = pull_one(env_grad_one)
    back_both = fold_grads(pos_grad_two[own_count:] + pos_grad_one[own_count:])
    pos_total = (pos_grad_two[:own_count] + pos_grad_one[:own_count]).at[send_list].add(back_both)
    return (energies, -pos_total.T)


def solution(mesh):
    return jax.shard_map(
        local,
        mesh=mesh,
        in_specs=(
            P(None, ("groups", "gx", "gy", "gz")),
            P(("groups", "gx", "gy", "gz"), None),
            P(("groups", "gx", "gy", "gz"), None),
            P(("groups", "gx", "gy", "gz"), None),
            P(("groups", "gx", "gy", "gz")),
            P(),
            P(),
            P(),
            P(),
            P(),
        ),
        out_specs=(P(("groups", "gx", "gy", "gz")), P(None, ("groups", "gx", "gy", "gz"))),
        check_vma=False,
    )
```

profile of v0, /device:TPU:0, one launch (start us, length us, event | category | flops | bytes accessed | tf_op | source)
XLA Modules:
  0.0 1360.1 jit_solution(10986529253583077351)
XLA Ops:
  42.2 291.8 %while.200 = (s32[]{:T(128)}, f32[352,640]{1,0:T(8,128)}, s32[5,512,1]{1,2,0:T(1,128)}, s32[5,512,1]{1,2,0:T(1,128)}, f32[5,512,3]{1,2,0:T(4,128)}, /*index=5*/f...) while((s32[]{:T(128)}, f32[352,640]{1,0:T(8,128)}, ...), condition=%wide.region_3.4_spmd.clone.clone, body=%wide.region_0.3_spmd.clone.clone.sunk | while | flops 130610712 | bytes 15955989 | solution.py:146
  74.0 6.1 scatter_custom_fusion.47
  132.2 6.1 scatter_custom_fusion.47
  190.6 6.1 scatter_custom_fusion.47
  249.0 6.1 scatter_custom_fusion.47
  307.3 6.1 scatter_custom_fusion.47
  342.8 4.8 collective-permute-done.6
  351.9 6.9 collective-permute-done.8
  358.8 3.5 collective-permute-done.9
  408.0 271.2 %while.201 = (s32[]{:T(128)}, f32[352,640]{1,0:T(8,128)}, s32[5,512,1]{1,2,0:T(1,128)}, s32[5,512,1]{1,2,0:T(1,128)}, f32[5,512,3]{1,2,0:T(4,128)}, /*index=5*/f...) while((s32[]{:T(128)}, f32[352,640]{1,0:T(8,128)}, ...), condition=%wide.region_12.13_spmd.clone.clone, body=%wide.region_9.12_spmd.clone.clone.sunk | while | flops 130610712 | bytes 15948641 | solution.py:146
  440.2 6.1 scatter_custom_fusion.49
  494.3 6.1 scatter_custom_fusion.49
  548.6 6.1 scatter_custom_fusion.49
  602.9 6.1 scatter_custom_fusion.49
  657.1 6.1 scatter_custom_fusion.49
  683.4 3.8 collective-permute-start.19
  687.1 5.0 collective-permute-done.18
  695.6 6.9 collective-permute-done.20
  702.4 3.8 collective-permute-done.21
  736.4 310.4 %while.202 = (s32[]{:T(128)}, f32[352,3]{1,0:T(8,128)}, f32[352,64]{1,0:T(8,128)S(1)}, f32[352,64]{1,0:T(8,128)S(1)}, f32[352,640]{1,0:T(8,128)S(1)}, /*index=5*...) while((s32[]{:T(128)}, f32[352,3]{1,0:T(8,128)}, ...), condition=%wide.region_28.29_spmd.clone.clone, body=%wide.region_18.28_spmd.clone.clone.sunk | while | flops 131967040 | bytes 34877364 | solution.py:146
  770.2 3.3 fusion.341
  795.4 3.3 scatter_fusion
  799.6 3.3 scatter_fusion.2
  803.0 3.3 scatter_fusion.1
  830.3 3.3 fusion.341
  855.5 3.3 scatter_fusion
  859.7 3.3 scatter_fusion.2
  863.1 3.3 scatter_fusion.1
  890.4 3.3 fusion.341
  915.6 3.3 scatter_fusion
  919.7 3.3 scatter_fusion.2
  923.1 3.3 scatter_fusion.1
  950.4 3.3 fusion.341
  975.7 3.3 scatter_fusion
  979.8 3.3 scatter_fusion.2
  983.2 3.3 scatter_fusion.1
  1010.5 3.3 fusion.341
  1035.7 3.3 scatter_fusion
  1039.9 3.3 scatter_fusion.2
  1043.2 3.3 scatter_fusion.1
  1052.5 3.3 collective-permute-start.31
  1071.0 3.9 collective-permute-start.37
  1086.5 251.5 %while.203 = (s32[]{:T(128)}, f32[352,3]{1,0:T(8,128)}, f32[352,640]{1,0:T(8,128)S(1)}, s32[5,512,1]{1,2,0:T(1,128)}, s32[5,512,1]{1,2,0:T(1,128)}, /*index=5*/f...) while((s32[]{:T(128)}, f32[352,3]{1,0:T(8,128)}, ...), condition=%wide.region_40.41_spmd.clone.clone, body=%wide.region_32.40_spmd.clone.clone.sunk | while | flops 131934272 | bytes 33689936 | solution.py:146
  1132.8 3.3 scatter_fusion.3
  1183.1 3.3 scatter_fusion.3
  1233.4 3.3 scatter_fusion.3
  1283.7 3.3 scatter_fusion.3
  1334.0 3.3 scatter_fusion.3
  (2052 shorter events, 1077.5 us)
Async XLA Ops:
  3.7 6.8 collective-permute-start
  6.8 3.7 collective-permute-start.1
  10.5 3.8 collective-permute-start.2
  12.2 3.7 collective-permute-start.3
  16.0 4.2 collective-permute-start.4
  16.1 4.1 collective-permute-start.5
  338.6 8.9 collective-permute-start.6
  340.0 9.7 collective-permute-start.7
  349.8 9.0 collective-permute-start.8
  350.4 11.8 collective-permute-start.9
  362.4 1.8 collective-permute-start.10
  362.5 2.2 collective-permute-start.11
  374.5 5.5 collective-permute-start.12
  376.7 3.7 collective-permute-start.13
  380.4 3.8 collective-permute-start.14
  380.9 3.7 collective-permute-start.15
  384.7 1.3 collective-permute-start.16
  384.7 1.4 collective-permute-start.17
  683.3 8.9 collective-permute-start.18
  683.4 10.0 collective-permute-start.19
  693.5 8.9 collective-permute-start.20
  695.1 11.1 collective-permute-start.21
  706.4 1.8 collective-permute-start.22
  706.5 2.2 collective-permute-start.23
  719.4 6.0 collective-permute-start.24
  722.5 4.1 collective-permute-start.25
  726.6 4.7 collective-permute-start.26
  728.1 4.4 collective-permute-start.27
  732.7 1.5 collective-permute-start.28
  732.7 1.6 collective-permute-start.29
  1051.9 5.9 collective-permute-start.30
  1052.5 5.3 collective-permute-start.31
  1057.9 4.8 collective-permute-start.32
  1060.7 4.1 collective-permute-start.33
  1064.8 1.3 collective-permute-start.34
  1064.9 1.4 collective-permute-start.35
  1070.8 6.0 collective-permute-start.36
  1071.0 5.9 collective-permute-start.37
  1076.9 5.0 collective-permute-start.38
  1077.5 5.3 collective-permute-start.39
  1082.9 1.5 collective-permute-start.40
  1083.0 1.6 collective-permute-start.41
  1341.6 5.9 collective-permute-start.42
  1343.5 4.6 collective-permute-start.43
  1348.1 4.3 collective-permute-start.44
  1350.3 4.1 collective-permute-start.45
  1354.5 1.5 collective-permute-start.46
  1354.6 1.4 collective-permute-start.47
  (304 other events, 2512.2 us)
where the time goes:
time: 1390 us; the launch traced here: 1360 us
  local copies, waits for them, and re-layouts  692 us (50%)
  other arithmetic  377 us (27%)
  loops' own time  94 us (7%)
  waiting for transfers between devices  70.5 us (5%)
  matrix products  69.4 us (5%)
  starting transfers between devices  54.9 us (4%)
    dynamic_update_slice x160, local copies, waits for them, and re-layouts, layer_env(): lax.scan(one_group, start_env, (seg_groups, other_groups, base_groups))  153 us
    dynamic_update_slice x80, local copies, waits for them, and re-layouts, one_group(): lax.dynamic_update_slice_in_dim(environment, current + summed[member], fi...  116 us
    another operation x4, loops' own time, layer_env(): lax.scan(one_group, start_env, (seg_groups, other_groups, base_groups))  94 us
    dynamic_slice x100, local copies, waits for them, and re-layouts, layer_env(): lax.scan(one_group, start_env, (seg_groups, other_groups, base_groups))  77.8 us
    scatter-add x10, other arithmetic, one_group(): environment = environment.at[partner].add(contrib * parity[None, :])  60.9 us
    scatter-add x20, other arithmetic, one_group(): separation = pos_ext[partner] - pos_ext[centre]  56.3 us
    add_any x40, local copies, waits for them, and re-layouts, one_group(): current = lax.dynamic_slice_in_dim(environment, first_row, SEG, 0)  55 us
    ppermute x24, waiting for transfers between devices, extended_2(): lax.ppermute(lax.slice_in_dim(block, block.shape[dim] - width, None, axis...  47.8 us
  transfers between devices with their start and end apart: 48, of which 41 were waited for; matrix products, arithmetic and copies ran while one was open for 1% of the time, Pallas kernels for 0%

commit v1 on v0

v1 whole, which is shorter than its diff:
```python
from functools import partial
import math

import jax
import jax.numpy as jnp
import numpy as np
from jax import lax
from jax.experimental import pallas as pl
from jax.experimental.pallas import tpu as pltpu
from jax.sharding import PartitionSpec as P

CH = 64
SEG = 32
ATOMS = 128
NP = 512
GPAD = 256
AXES = ("groups", "gx", "gy", "gz")
ORDER = [1, 2, 3, 0, 4, 5, 6, 7, 8, 9]
ODD = 3 * CH
WIDE = 10 * CH
ROOT2 = math.sqrt(2.0)
F32 = jnp.float32
BF16 = jnp.bfloat16
MESH_ID = pl.DeviceIdType.MESH


def axis_side(padded):
    if padded == 0:
        return (-1, 1)
    if padded == 3:
        return (1, 0)
    return (0, padded - 1)


def axis_options(size):
    if size == 2:
        return [(0, (1, 2)), (1, (0, 3))]
    return [(0, (1, 2)), (-1, (0,)), (1, (3,))]


def neighbour_groups(sizes, ghost):
    number = {}
    for p in range(4):
        for q in range(4):
            for r in range(4):
                if not (p in (1, 2) and q in (1, 2) and r in (1, 2)):
                    number[(p, q, r)] = len(number)
    groups, slots = [], []
    for ox, ps in axis_options(sizes[0]):
        for oy, qs in axis_options(sizes[1]):
            for oz, rs in axis_options(sizes[2]):
                if ox == 0 and oy == 0 and oz == 0:
                    continue
                first = len(slots) * ghost
                slots += [(p, q, r) for p in ps for q in qs for r in rs]
                groups.append(((ox, oy, oz), first, len(slots) * ghost - first))
    rows = np.full((ATOMS + GPAD,), -5, np.int32)
    rows[:ATOMS] = np.arange(ATOMS)
    shift = np.zeros((GPAD, 128), np.float32)
    pick = np.zeros((8 * ghost, GPAD), np.float32)
    for at, key in enumerate(slots):
        sides = [axis_side(t) for t in key]
        slot = (sides[0][1] * 2 + sides[1][1]) * 2 + sides[2][1]
        for g in range(ghost):
            j = at * ghost + g
            rows[ATOMS + j] = ATOMS + number[key] * ghost + g
            shift[j, CH : CH + 3] = [s[0] for s in sides]
            pick[slot * ghost + g, j] = 1.0
    tab = np.repeat(rows[:, None], 128, axis=1)
    return groups, tab, shift, pick


def split(x):
    hi = x.astype(BF16)
    return hi, (x - hi.astype(F32)).astype(BF16)


def nn(a, b):
    return jnp.dot(a, b, preferred_element_type=F32)


def nt(a, b):
    return lax.dot_general(a, b, (((1,), (1,)), ((), ())), preferred_element_type=F32)


def nn_exact(a, b):
    return jnp.dot(a, b, precision=lax.Precision.HIGHEST, preferred_element_type=F32)


def nt_exact(a, b):
    return lax.dot_general(
        a, b, (((1,), (1,)), ((), ())), precision=lax.Precision.HIGHEST, preferred_element_type=F32
    )


def sigmoid(x):
    return 1.0 / (1.0 + jnp.exp(-x))


def kernel_body(
    groups, sizes, nblk, ghost_rows,
    pos_ref, feat_ref, seg_ref, oth_ref, send_ref, rad_ref, radt_ref, wa_ref, wb_ref, uw_ref, read_ref,
    tab_ref, shift_ref, pick_ref, base_ref,
    en_ref, force_ref,
    oh, eo, do, geo, bas, bf1, bf2, lhs, con_hi, con_lo, acc_o, acc_e, acc_g, gt_hi, gt_lo, acc_b,
    x0, pospad, xext, genv, small_out, small_in, wide_out, wide_in, send_sem, recv_sem,
):
    me = [lax.axis_index(a) for a in AXES]

    def target(offset, sign):
        ids = [me[0]]
        for k in range(3):
            ids.append(lax.rem(me[k + 1] + sign * offset[k] + sizes[k], sizes[k]))
        return tuple(ids)

    barrier = pltpu.get_barrier_semaphore()
    for offset, first, count in groups:
        pl.semaphore_signal(barrier, inc=1, device_id=target(offset, 1), device_id_type=MESH_ID)

    def exchange(k, src, dst, sign):
        copies = []
        for n, (offset, first, count) in enumerate(groups):
            copies.append(
                pltpu.make_async_remote_copy(
                    src_ref=src.at[pl.ds(first, count)],
                    dst_ref=dst.at[pl.ds(first, count)],
                    send_sem=send_sem.at[k, n],
                    recv_sem=recv_sem.at[k, n],
                    device_id=target(offset, sign),
                    device_id_type=MESH_ID,
                )
            )
        for copy in copies:
            copy.start()
        return copies

    def finish(copies):
        for copy in copies:
            copy.wait()

    chunks = nblk * 128 // NP

    pospad[...] = jnp.zeros_like(pospad)
    pospad[0:3, :] = pos_ref[...]
    eye = (
        lax.broadcasted_iota(jnp.int32, (128, 128), 0) == lax.broadcasted_iota(jnp.int32, (128, 128), 1)
    ).astype(F32)
    x0[:, 0:CH] = feat_ref[...]
    x0[:, CH:128] = nt_exact(eye, pospad[...])
    slots = send_ref.shape[1]
    sot = (lax.broadcasted_iota(jnp.int32, (ATOMS, slots), 0) == send_ref[...]).astype(BF16)
    srt_f = nn(sot, pick_ref[...].astype(BF16))
    srt = srt_f.astype(BF16)
    sr = jnp.transpose(srt_f).astype(BF16)

    def pick_rows(x):
        hi, lo = split(x)
        return nn(sr, hi) + nn(sr, lo)

    def add_back(x):
        hi, lo = split(x)
        return nn(srt, hi) + nn(srt, lo)

    mid = (x0[...] - x0[...].astype(BF16).astype(F32)).astype(BF16).astype(F32)
    low = x0[...] - x0[...].astype(BF16).astype(F32) - mid
    small_out[0] = (pick_rows(x0[...]) + nn(sr, low.astype(BF16)))[:ghost_rows]
    pl.semaphore_wait(barrier, len(groups))
    moving = exchange(0, small_out.at[0], small_in.at[0], -1)

    def build(b, carry):
        other = oth_ref[pl.ds(b, 1), :]
        centre = jnp.where(other >= 0, seg_ref[pl.ds(b, 1), :] + base_ref[pl.ds(b, 1), :], -1)
        sl = pl.ds(pl.multiple_of(b * 128, 128), 128)
        c = (lax.broadcasted_iota(jnp.int32, (ATOMS, 128), 0) == centre).astype(F32)
        p = (tab_ref[...] == other).astype(F32)
        oh[0:128, sl] = c.astype(BF16)
        oh[128:512, sl] = p.astype(BF16)
        eo[:, sl] = (c + p[0:128]).astype(BF16)
        do[:, sl] = (c - p[0:128]).astype(BF16)
        return carry

    lax.fori_loop(0, nblk, build, 0)
    finish(moving)

    sign_row = jnp.where(lax.broadcasted_iota(jnp.int32, (1, WIDE), 1) < ODD, -1.0, 1.0)
    pad_rows = GPAD - ghost_rows

    def fill_ext(own, ghosts, with_shift):
        xext[0:ATOMS, :] = own
        if with_shift:
            xext[ATOMS : ATOMS + ghost_rows, :] = ghosts + shift_ref[0:ghost_rows, :]
        else:
            xext[ATOMS : ATOMS + ghost_rows, :] = ghosts
        xext[ATOMS + ghost_rows :, :] = jnp.zeros((pad_rows, 128), F32)

    def make_lhs(layer):
        feats = xext[:, 0:CH]
        pa = nt_exact(wa_ref[layer], feats[0:ATOMS])
        pb = nt_exact(wb_ref[layer], feats)
        hi, lo = split(jnp.concatenate([pa, pb], axis=1))
        lhs[0:CH, :] = hi
        lhs[CH : 2 * CH, :] = lo
        if layer == 0:
            pick = (
                lax.broadcasted_iota(jnp.int32, (16, 128), 0) + CH
                == lax.broadcasted_iota(jnp.int32, (16, 128), 1)
            ) & (lax.broadcasted_iota(jnp.int32, (16, 128), 0) < 3)
            pt = nt_exact(pick.astype(F32), xext[...])
            both = jnp.concatenate([-pt[:, 0:ATOMS], pt], axis=1)
            p1 = both.astype(BF16)
            rest = both - p1.astype(F32)
            p2, p3 = split(rest)
            lhs[128:144, :] = p1
            lhs[144:160, :] = p2
            lhs[160:176, :] = p3

    def angular(ux, uy, uz):
        third = (ux * ux + uy * uy + uz * uz) * (1.0 / 3.0)
        return [
            None, ux, uy, uz, ux * ux - third, uy * uy - third, uz * uz - third,
            ROOT2 * ux * uy, ROOT2 * ux * uz, ROOT2 * uy * uz,
        ]

    def centres():
        return 0.5 * (lax.broadcasted_iota(jnp.int32, (8, 1), 0) + 1).astype(F32)

    def forward(layer, before_ref):
        acc_o[...] = jnp.zeros_like(acc_o)
        acc_e[...] = jnp.zeros_like(acc_e)
        acc_g[...] = jnp.zeros_like(acc_g)

        def chunk(i, carry):
            sl = pl.ds(pl.multiple_of(i * NP, NP), NP)
            cp = oh[:, sl]
            if layer == 0:
                got = nn(lhs[...], cp)
                sep = got[128:136] + got[144:152] + got[160:168]
                sx, sy, sz = sep[0:1], sep[1:2], sep[2:3]
                dist = jnp.sqrt(sx * sx + sy * sy + sz * sz + 0.25)
                inv = 1.0 / dist
                ux, uy, uz = sx * inv, sy * inv, sz * inv
                scaled = dist * 0.25
                fall = 1.0 - scaled * scaled
                envelope = fall * fall
                geo[0:1, sl] = ux
                geo[1:2, sl] = uy
                geo[2:3, sl] = uz
                geo[3:4, sl] = dist
                geo[4:5, sl] = inv
                geo[5:6, sl] = envelope
                geo[6:7, sl] = -scaled * fall
                step = (dist - centres()) * 2.0
                basis = jnp.exp(-step * step)
                bas[:, sl] = basis
            else:
                got = nn(lhs[0:128, :], cp)
                ux, uy, uz = geo[0:1, sl], geo[1:2, sl], geo[2:3, sl]
                envelope = geo[5:6, sl]
                basis = bas[:, sl]
            before = nn_exact(rad_ref[layer], basis) + got[0:CH] + got[CH : 2 * CH]
            before_ref[:, sl] = before
            weight = envelope * (before * sigmoid(before))
            ang = angular(ux, uy, uz)
            for at, m in enumerate(ORDER):
                value = weight if m == 0 else weight * ang[m]
                hi, lo = split(value)
                con_hi[at * CH : (at + 1) * CH, :] = hi
                con_lo[at * CH : (at + 1) * CH, :] = lo
            d, e, g = do[:, sl], eo[:, sl], oh[256:512, sl]
            acc_o[...] += nt(d, con_hi[0:ODD]) + nt(d, con_lo[0:ODD])
            acc_e[...] += nt(e, con_hi[ODD:]) + nt(e, con_lo[ODD:])
            acc_g[...] += nt(g, con_hi[...]) + nt(g, con_lo[...])
            return carry

        lax.fori_loop(0, chunks, chunk, 0)

    def fold_env(k, w):
        wide_out[w] = (acc_g[...] * sign_row)[:ghost_rows]
        finish(exchange(k, wide_out.at[w], wide_in.at[w], 1))
        own = jnp.concatenate([acc_o[...], acc_e[...]], axis=1)
        arrived = jnp.concatenate([wide_in[w], jnp.zeros((pad_rows, WIDE), F32)], axis=0)
        return own + add_back(arrived)

    def part(env, at):
        return env[:, at * CH : (at + 1) * CH]

    def update(h, env, layer):
        square = [part(env, at) * part(env, at) for at in range(10)]
        vec = 0.1 * (square[0] + square[1] + square[2])
        ten = 0.1 * (square[4] + square[5] + square[6] + square[7] + square[8] + square[9])
        joined = jnp.concatenate([0.25 * part(env, 3), vec, ten], axis=1)
        z = nt_exact(joined, uw_ref[layer])
        return h + z * sigmoid(z), z

    def env_grad(hbar, z, env, layer):
        s = sigmoid(z)
        zbar = hbar * (s * (1.0 + z * (1.0 - s)))
        jbar = nn_exact(zbar, uw_ref[layer])
        sb = 0.25 * jbar[:, 0:CH]
        vb = 0.2 * jbar[:, CH : 2 * CH]
        tb = 0.2 * jbar[:, 2 * CH :]
        pieces = [vb * part(env, at) for at in range(3)] + [sb]
        pieces += [tb * part(env, at) for at in range(4, 10)]
        return jnp.concatenate(pieces, axis=1)

    def spread_env(k, w, grad):
        wide_out[w] = pick_rows(grad)[:ghost_rows]
        moving = exchange(k, wide_out.at[w], wide_in.at[w], -1)
        hi, lo = split(jnp.transpose(grad))
        gt_hi[:, 0:ATOMS] = hi
        gt_lo[:, 0:ATOMS] = lo
        finish(moving)
        full = jnp.concatenate([wide_in[w] * sign_row, jnp.zeros((pad_rows, WIDE), F32)], axis=0)
        hi, lo = split(jnp.transpose(full))
        gt_hi[:, ATOMS:] = hi
        gt_lo[:, ATOMS:] = lo

    def backward(layer, before_ref):
        acc_b[...] = jnp.zeros_like(acc_b)

        def chunk(i, carry):
            sl = pl.ds(pl.multiple_of(i * NP, NP), NP)
            d, e, g = do[:, sl], eo[:, sl], oh[256:512, sl]
            go = (
                nn(gt_hi[0:ODD, 0:ATOMS], d) + nn(gt_lo[0:ODD, 0:ATOMS], d)
                + nn(gt_hi[0:ODD, ATOMS:], g) + nn(gt_lo[0:ODD, ATOMS:], g)
            )
            ge = (
                nn(gt_hi[ODD:, 0:ATOMS], e) + nn(gt_lo[ODD:, 0:ATOMS], e)
                + nn(gt_hi[ODD:, ATOMS:], g) + nn(gt_lo[ODD:, ATOMS:], g)
            )
            ux, uy, uz = geo[0:1, sl], geo[1:2, sl], geo[2:3, sl]
            dist, inv, envelope, fall = geo[3:4, sl], geo[4:5, sl], geo[5:6, sl], geo[6:7, sl]
            basis = bas[:, sl]
            before = before_ref[:, sl]
            s = sigmoid(before)
            act = before * s
            weight = envelope * act
            ang = angular(ux, uy, uz)
            wbar = None
            abar = [None] * 10
            for at, m in enumerate(ORDER):
                gm = go[at * CH : (at + 1) * CH] if at < 3 else ge[(at - 3) * CH : (at - 2) * CH]
                term = gm if m == 0 else gm * ang[m]
                wbar = term if wbar is None else wbar + term
                if m:
                    abar[m] = jnp.sum(weight * gm, axis=0, keepdims=True)
            envbar = jnp.sum(wbar * act, axis=0, keepdims=True)
            bbar = envelope * wbar * (s * (1.0 + before * (1.0 - s)))
            kbar = nn_exact(radt_ref[layer], bbar)
            step = (dist - centres()) * 2.0
            dbar = jnp.sum(kbar * basis * step, axis=0, keepdims=True) * -4.0 + envbar * fall
            third = (abar[4] + abar[5] + abar[6]) * (1.0 / 3.0)
            xb = abar[1] + 2.0 * ux * (abar[4] - third) + ROOT2 * (uy * abar[7] + uz * abar[8])
            yb = abar[2] + 2.0 * uy * (abar[5] - third) + ROOT2 * (ux * abar[7] + uz * abar[9])
            zb = abar[3] + 2.0 * uz * (abar[6] - third) + ROOT2 * (ux * abar[8] + uy * abar[9])
            dbar = dbar - (xb * ux + yb * uy + zb * uz) * inv
            rx, ry, rz = xb * inv + ux * dbar, yb * inv + uy * dbar, zb * inv + uz * dbar
            r16 = jnp.concatenate([rx, ry, rz, jnp.zeros((13, NP), F32)], axis=0)
            r_hi, r_lo = split(r16)
            con_hi[128:144, :] = r_hi
            con_hi[144:160, :] = r_lo
            if layer == 1:
                b_hi, b_lo = split(bbar)
                con_hi[0:CH, :] = b_hi
                con_hi[CH : 2 * CH, :] = b_lo
            acc_b[...] += nt(oh[:, sl], con_hi[0:256, :])
            return carry

        lax.fori_loop(0, chunks, chunk, 0)

    def pos_rows():
        both = acc_b[:, 128:144] + acc_b[:, 144:160]
        return both[128:256] - both[0:128], both[256 : 256 + ghost_rows]

    fill_ext(x0[...], small_in[0], True)
    make_lhs(0)
    forward(0, bf1)
    genv[0] = fold_env(1, 0)
    h1, z1 = update(feat_ref[...], genv[0], 0)
    h1w = jnp.concatenate([h1, jnp.zeros((ATOMS, CH), F32)], axis=1)
    small_out[1] = pick_rows(h1w)[:ghost_rows]
    finish(exchange(2, small_out.at[1], small_in.at[1], -1))
    fill_ext(h1w, small_in[1], False)
    make_lhs(1)
    forward(1, bf2)
    genv[1] = fold_env(3, 1)
    h2, z2 = update(h1, genv[1], 1)
    en_ref[...] = nt_exact(read_ref[...], h2)
    hbar2 = jnp.broadcast_to(read_ref[...], (ATOMS, CH))
    spread_env(4, 2, env_grad(hbar2, z2, genv[1], 1))
    con_hi[...] = jnp.zeros_like(con_hi)
    backward(1, bf2)
    pos_own2, pos_ghost2 = pos_rows()
    ab = acc_b[:, 0:CH] + acc_b[:, CH : 2 * CH]
    hb = nn_exact(ab[128:512], wb_ref[1])
    small_out[2] = jnp.concatenate(
        [hb[ATOMS : ATOMS + ghost_rows], jnp.zeros((ghost_rows, CH), F32)], axis=1
    )
    moving = exchange(5, small_out.at[2], small_in.at[2], 1)
    own_bar = hbar2 + hb[0:ATOMS] + nn_exact(ab[0:128], wa_ref[1])
    finish(moving)
    arrived = jnp.concatenate([small_in[2], jnp.zeros((pad_rows, 128), F32)], axis=0)
    own_bar = own_bar + add_back(arrived)[:, 0:CH]
    spread_env(6, 3, env_grad(own_bar, z1, genv[0], 0))
    backward(0, bf1)
    pos_own1, pos_ghost1 = pos_rows()
    small_out[3] = jnp.concatenate(
        [pos_ghost1 + pos_ghost2, jnp.zeros((ghost_rows, 112), F32)], axis=1
    )
    finish(exchange(7, small_out.at[3], small_in.at[3], 1))
    arrived = jnp.concatenate([small_in[3], jnp.zeros((pad_rows, 128), F32)], axis=0)
    total = add_back(arrived)[:, 0:16] + pos_own1 + pos_own2
    pick16 = (
        lax.broadcasted_iota(jnp.int32, (8, 16), 0) == lax.broadcasted_iota(jnp.int32, (8, 16), 1)
    ).astype(F32)
    force_ref[...] = -nt_exact(pick16, total)[0:3]


def local(sizes, positions, feats, seg, oth, send, rad, wa, wb, uw, read):
    ghost = send.shape[0] // 8
    ghost_rows = 56 * ghost
    nblk = seg.shape[0]
    groups, tab, shift, pick = neighbour_groups(sizes, ghost)
    base = np.repeat((np.arange(nblk) * (ATOMS - SEG) // (nblk - 1)).astype(np.int32)[:, None], 128, axis=1)
    pairs = nblk * 128
    vm = pltpu.VMEM
    spec = pl.BlockSpec(memory_space=pltpu.VMEM)
    energies, forces = pl.pallas_call(
        partial(kernel_body, groups, sizes, nblk, ghost_rows),
        out_shape=(jax.ShapeDtypeStruct((1, ATOMS), F32), jax.ShapeDtypeStruct((3, ATOMS), F32)),
        in_specs=[spec] * 15,
        out_specs=(spec, spec),
        scratch_shapes=[
            vm((512, pairs), BF16),
            vm((ATOMS, pairs), BF16),
            vm((ATOMS, pairs), BF16),
            vm((8, pairs), F32),
            vm((8, pairs), F32),
            vm((CH, pairs), F32),
            vm((CH, pairs), F32),
            vm((176, 512), BF16),
            vm((WIDE, NP), BF16),
            vm((WIDE, NP), BF16),
            vm((ATOMS, ODD), F32),
            vm((ATOMS, WIDE - ODD), F32),
            vm((GPAD, WIDE), F32),
            vm((WIDE, ATOMS + GPAD), BF16),
            vm((WIDE, ATOMS + GPAD), BF16),
            vm((512, 256), F32),
            vm((ATOMS, 128), F32),
            vm((CH, ATOMS), F32),
            vm((ATOMS + GPAD, 128), F32),
            vm((2, ATOMS, WIDE), F32),
            vm((4, ghost_rows, 128), F32),
            vm((4, ghost_rows, 128), F32),
            vm((4, ghost_rows, WIDE), F32),
            vm((4, ghost_rows, WIDE), F32),
            pltpu.SemaphoreType.DMA((8, len(groups))),
            pltpu.SemaphoreType.DMA((8, len(groups))),
        ],
        compiler_params=pltpu.CompilerParams(
            collective_id=0, has_side_effects=True, vmem_limit_bytes=48 * 1024 * 1024
        ),
        name="pair_potential",
    )(
        positions, feats, seg, oth, send.reshape(1, -1), rad, jnp.swapaxes(rad, 1, 2), wa, wb, uw,
        read.reshape(1, -1), jnp.asarray(tab), jnp.asarray(shift), jnp.asarray(pick), jnp.asarray(base),
    )
    return energies.reshape(-1), forces


def solution(mesh):
    split_all = AXES
    sizes = tuple(mesh.shape[a] for a in AXES[1:])
    return jax.shard_map(
        partial(local, sizes),
        mesh=mesh,
        in_specs=(
            P(None, split_all),
            P(split_all, None),
            P(split_all, None),
            P(split_all, None),
            P(split_all),
            P(),
            P(),
            P(),
            P(),
            P(),
        ),
        out_specs=(P(split_all), P(None, split_all)),
        check_vma=False,
    )
```

time: 1390 us -> 111 us (0.08); the launches traced: 1360 us -> 111 us
  local copies, waits for them, and re-layouts: 692 us -> 8.44 us
  other arithmetic: 377 us -> 0 us
  Pallas kernels: 0 us -> 102 us
  loops' own time: 94 us -> 0 us
  waiting for transfers between devices: 70.5 us -> 0 us
  matrix products: 69.4 us -> 0 us
  starting transfers between devices: 54.9 us -> 0 us
    dynamic_update_slice x240 -> x0, local copies, waits for them, and re-layouts: 269 us -> none  [the longest x160 153 us: layer_env(): lax.scan(one_group, start_env, (seg_groups, other_groups, base_groups))]
    scatter-add x44 -> x0, other arithmetic: 154 us -> none  [the longest x10 60.9 us: one_group(): environment = environment.at[partner].add(contrib * parity[None, :])]
    gather x120 -> x0, local copies, waits for them, and re-layouts: 103 us -> none  [the longest x20 34.5 us: one_group(): environment = environment.at[partner].add(contrib * parity[None, :])]
    pallas_call x0 -> x1, Pallas kernels: none -> 102 us  [local(): pl.pallas_call(partial(kernel_body, groups, sizes, nblk, ghost_rows), out...]
    another operation x4 -> x0, loops' own time: 94 us -> none  [layer_env(): lax.scan(one_group, start_env, (seg_groups, other_groups, base_groups))]
    dynamic_slice x100 -> x0, local copies, waits for them, and re-layouts: 77.8 us -> none  [layer_env(): lax.scan(one_group, start_env, (seg_groups, other_groups, base_groups))]
    ppermute x48 -> x0, waiting for transfers between devices: 70.5 us -> none  [the longest x24 47.8 us: extended_2(): lax.ppermute(lax.slice_in_dim(block, block.shape[dim] - width, None, axis...]
    dot_general x51 -> x0, matrix products: 69.4 us -> none  [the longest x20 40.7 us: one_group(): jnp.einsum('bps,bpk->bsk', selector, contrib.reshape(4, 128, 10 * CH), pr...]
  transfers between devices with their start and end apart: 48 -> 0, of which waited for: 41 -> 0; matrix products, arithmetic and copies ran while one was open for 1% -> 0% of each run, Pallas kernels for 0% -> 0%
where the time goes in v1:
time: 111 us
  Pallas kernels  102 us (92%)
  local copies, waits for them, and re-layouts  8.44 us (8%)
    pallas_call x1, Pallas kernels, local(): pl.pallas_call(partial(kernel_body, groups, sizes, nblk, ghost_rows), out...  102 us
    unnamed x30, local copies, waits for them, and re-layouts  8.44 us

profile of v1, /device:TPU:0, one launch (start us, length us, event | category | flops | bytes accessed | tf_op | source)
XLA Modules:
  0.0 110.8 jit_solution(14326052963965397468)
XLA Ops:
  0.6 0.0 copy-start.1
  0.6 0.9 copy.16.feat_ref
  1.5 0.0 copy-start.5
  1.5 0.0 copy-start.6
  1.6 0.0 copy-start.10
  1.6 0.0 copy-start.11
  1.6 0.0 copy-start.12
  1.6 0.8 copy.17.rad_ref
  2.4 0.0 copy-done.1
  2.4 0.0 copy-done.5
  2.4 0.0 copy-done.6
  2.4 0.0 copy-done.10
  2.4 0.0 copy-done.11
  2.5 0.0 copy-done.12
  2.5 0.0 copy-start
  2.5 0.9 copy-done
  3.4 0.0 copy-start.2
  3.4 0.9 copy-done.2
  4.3 0.0 copy-start.3
  4.3 0.8 copy-done.3
  5.1 0.0 copy-start.4
  5.1 0.8 copy-done.4
  6.0 0.0 copy-start.7
  6.0 0.7 copy-done.7
  6.7 0.0 copy-start.8
  6.7 0.7 copy-done.8
  7.4 0.0 copy-start.9
  7.4 0.7 copy-done.9
  8.1 101.6 %pair_potential.1 = (f32[1,128]{1,0:T(1,128)S(1)}, f32[3,128]{1,0:T(4,128)S(1)}) custom-call(f32[3,128]{1,0:T(4,128)S(1)} %copy-done.10, f32[128,64]{1,0:T(8,128)S(1)} %copy.16.feat_ref, s32[20,128]{1,0:T(8,128)S(1)} %copy-done.7, s32[20,128]{1,0:T(8,128)S(1)} %copy-done.8, s32[1,32]{1,0:T(1,128)S(1)} %bitcast.5, f32[2,64,8]{2,1,0:T(8,128)S(1)} %copy.17.rad_ref, ...), custom_call_target="tpu_custom_call" | custom-call | tf_op jit(solution)/shard_map/pair_potential/pallas_call | solution.py:429
  109.7 0.5 copy.20
  110.2 0.6 copy.21
Async XLA Ops:
  0.6 1.8 %copy-start.1 = (f32[2,64,192]{2,1,0:T(8,128)S(1)}, f32[2,64,192]{2,1,0:T(8,128)}, u32[]{:S(2)}) copy-start(f32[2,64,192]{2,1,0:T(8,128)} %uw_ref.1) | copy-start | bytes 294916
  1.5 0.9 copy-start.5
  1.5 0.9 copy-start.6
  1.6 0.9 copy-start.10
  1.6 0.9 copy-start.11
  1.6 0.9 copy-start.12
  2.5 0.9 copy-start
  3.4 0.9 copy-start.2
  4.3 0.8 copy-start.3
  5.1 0.8 copy-start.4
  6.0 0.7 copy-start.7
  6.7 0.7 copy-start.8
  7.4 0.7 copy-start.9
